TPU v7x, 32 devices: a whole 2x2x4 slice. The times are simulated.
32 devices in a mesh: cells: 8 (over z, x), ens: 4 (over y, core).
Axes of the slice: x: 2, y: 2, z: 4, core: 2. Of those that a mesh axis runs over, the one named last changes fastest.
Arguments:
- state_mean: float32 [16384], P('cells'), may hold values from -6 to 6
- state_pert: float32 [256, 16384], P('ens', 'cells'), may hold values from -6 to 6
- obs_value: float32 [4, 512], P(None, 'cells'), may hold values from -10 to 10
- obs_error: float32 [4, 512], P(None, 'cells'), may hold values from 0.1 to 2
- obs_cell: int32 [4, 512], replicated, may hold values from 0 to 16383, as said below
- block_obs: int32 [4, 32, 96], P(None, 'cells'), may hold values from 0 to 511, as said below
- block_count: int32 [4, 32], P(None, 'cells'), may hold values from 0 to 96, as said below
- batch_order: int32 [4], replicated, may hold values from 0 to 3, each once
Outputs:
- mean_out: float32 [16384], P('cells')
- pert_out: float32 [256, 16384], P('ens', 'cells')
Inputs may be any that keep to these rules, and one draw needn't show every extreme that they name: `obs_cell`: each batch's entries are ordered by owner, 64 to an owner, each owner's in nondecreasing blocks; at most 32 observations of a batch lie in one block and at most 16 of one owner's in the cells of one index of cells, both reached in every batch. `block_obs`: entries l < block_count[b, B] are the observations of batch b lying in blocks B - 1, B and B + 1, in order; later entries are arbitrary observations of the batch. `block_count`: the largest is reached in every batch.
All inputs are finite; a program needn't handle non-finite values.
Results may differ from a plain program's by a relative error of at most 0.0001.
Values sent between devices are 32-bit elements; how exact they have to be, the bound alone decides.
A program may use at most 64 MiB of HBM per device.

v0:
```python
import jax
import jax.numpy as jnp
from jax import lax
from jax.sharding import PartitionSpec as P

MEMBERS = 256
CELL_BLK = 512


def taper_weight(distance, radius):
    fraction = distance / radius
    inside = (1.0 - fraction) * (1.0 - fraction) * (1.0 + 2.0 * fraction)
    return jnp.where(fraction < 1.0, inside, jnp.zeros_like(inside))


def group_ranks(source, owners, per_owner):
    src_table = source.reshape(owners, per_owner)
    matches = src_table[:, :, None] == src_table[:, None, :]
    earlier = jnp.arange(per_owner)[None, :] < jnp.arange(per_owner)[:, None]
    return (src_table, jnp.sum((matches & earlier[None]).astype(jnp.int32), axis=2))


def apply_panel(sel_panel, mem_rows, blocks, list_ids):
    blk_rows = blocks.shape[1]
    list_len = list_ids.shape[0]
    sel_anoms = sel_panel[:mem_rows].reshape(mem_rows, blk_rows, list_len)
    innov_list = sel_panel[mem_rows].reshape(blk_rows, list_len)
    gain_list = sel_panel[mem_rows + 1].reshape(blk_rows, list_len)
    alpha_list = sel_panel[mem_rows + 2].reshape(blk_rows, list_len)
    return (sel_anoms, innov_list, gain_list, alpha_list)


def finish_update(
    cov_block,
    cell_grid,
    where_list,
    counts,
    list_ids,
    gain_list,
    innov_list,
    alpha_list,
    sel_anoms,
    blocks,
    mean_state,
):
    distance = jnp.abs(cell_grid[:, None, :] - where_list[:, :, None]).astype(jnp.float32)
    live_mask = (list_ids[None, :] < counts[:, None]).astype(jnp.float32)
    weight = (
        cov_block * taper_weight(distance, 2.0 * CELL_BLK) * (live_mask * gain_list)[:, :, None]
    )
    mean_next = mean_state + jnp.sum(weight * innov_list[:, :, None], axis=1).reshape(-1)
    update = jnp.einsum(
        "blc,mbl->mbc", weight * alpha_list[:, :, None], sel_anoms, precision=lax.Precision.HIGHEST
    )
    return (mean_next, (blocks - update).reshape(blocks.shape[0], -1))


def shards(
    state_mean, state_pert, obs_value, obs_error, obs_cell, block_obs, block_count, batch_order
):
    cell_devs = lax.axis_size("cells")
    my_index = lax.axis_index("cells")
    cell_per = state_mean.shape[0]
    mem_per = state_pert.shape[0]
    blk_per = block_obs.shape[1]
    list_len = block_obs.shape[2]
    obs_per = obs_value.shape[1]
    slot_span = list_len // 3
    capacity = (blk_per * slot_span + cell_devs - 1) // cell_devs
    first_cell = my_index * cell_per
    list_ids = jnp.arange(list_len, dtype=jnp.int32)
    slot_ids = jnp.arange(capacity, dtype=jnp.int32)
    local_cells = first_cell + jnp.arange(cell_per, dtype=jnp.int32).reshape(blk_per, CELL_BLK)
    mean_state = state_mean
    pert_state = state_pert
    for step_index in range(obs_cell.shape[0]):
        batch_id = batch_order[step_index]
        obs_where = lax.dynamic_index_in_dim(obs_cell, batch_id, 0, keepdims=False)
        source = obs_where // cell_per
        src_table, slot_rank = group_ranks(source, cell_devs, obs_per)
        picked = (src_table == my_index)[:, None, :] & (
            slot_rank[:, None, :] == slot_ids[None, :, None]
        )
        local_of = (obs_where - first_cell).reshape(cell_devs, obs_per)
        keep_mask = jnp.any(picked, axis=2).reshape(-1).astype(jnp.float32)
        cell_pick = jnp.sum(jnp.where(picked, local_of[:, None, :], 0), axis=2).reshape(-1)
        send_pert = jnp.take(pert_state, cell_pick, axis=1) * keep_mask[None, :]
        send_mean = (jnp.take(mean_state, cell_pick) * keep_mask)[None, :]
        recv_pert, recv_mean = (
            lax.all_to_all(send_pert, "cells", split_axis=1, concat_axis=1, tiled=True),
            lax.all_to_all(send_mean, "cells", split_axis=1, concat_axis=1, tiled=True),
        )
        my_src = lax.dynamic_index_in_dim(src_table, my_index, 0, keepdims=False)
        my_rank = lax.dynamic_index_in_dim(slot_rank, my_index, 0, keepdims=False)
        column = my_src * capacity + my_rank
        values = jnp.take(recv_pert, column, axis=1)
        base_mean = jnp.take(recv_mean[0], column)
        first_sum = lax.psum(jnp.sum(values, axis=0), "ens")
        col_shift = first_sum / MEMBERS
        anomaly = values - col_shift[None, :]
        spread = lax.psum(jnp.sum(anomaly * anomaly, axis=0), "ens") / (MEMBERS - 1)
        observed = lax.dynamic_index_in_dim(obs_value, batch_id, 0, keepdims=False)
        obs_var = lax.dynamic_index_in_dim(obs_error, batch_id, 0, keepdims=False)
        innovation = observed - (base_mean + col_shift)
        total_var = spread + obs_var
        gain_obs = 1.0 / total_var
        alpha_obs = 1.0 / (1.0 + jnp.sqrt(obs_var / total_var))
        panel = jnp.concatenate([anomaly, jnp.stack([innovation, gain_obs, alpha_obs])], axis=0)
        obs_lists = lax.dynamic_index_in_dim(block_obs, batch_id, 0, keepdims=False)
        counts = lax.dynamic_index_in_dim(block_count, batch_id, 0, keepdims=False)
        flat_list = obs_lists.reshape(-1)
        gathered = lax.all_gather(panel, "cells", axis=1, tiled=True)
        sel_panel = jnp.take(gathered, flat_list, axis=1)
        blocks = pert_state.reshape(mem_per, blk_per, CELL_BLK)
        sel_anoms, innov_list, gain_list, alpha_list = apply_panel(
            sel_panel, mem_per, blocks, list_ids
        )
        where_list = jnp.take(obs_where, flat_list).reshape(blk_per, list_len)
        partial_cov = jnp.einsum("mbl,mbc->blc", sel_anoms, blocks, precision=lax.Precision.HIGHEST)
        cov_block = lax.psum(partial_cov, "ens") / (MEMBERS - 1)
        mean_state, pert_state = finish_update(
            cov_block,
            local_cells,
            where_list,
            counts,
            list_ids,
            gain_list,
            innov_list,
            alpha_list,
            sel_anoms,
            blocks,
            mean_state,
        )
    return (mean_state, pert_state)


def solution(mesh):
    placed = (
        P("cells"),
        P("ens", "cells"),
        P(None, "cells"),
        P(None, "cells"),
        P(),
        P(None, "cells", None),
        P(None, "cells"),
        P(),
    )
    return jax.shard_map(
        shards,
        mesh=mesh,
        in_specs=placed,
        out_specs=(P("cells"), P("ens", "cells")),
        check_vma=False,
    )
```

profile of v0, /device:TPU:1, one launch (start us, length us, event | category | flops | bytes accessed | tf_op | source)
XLA Modules:
  0.0 462.1 jit_solution(12374676045079555902)
XLA Ops:
  21.6 6.4 %all-to-all-start.1 = ((f32[1,8,16]{2,0,1:T(1,128)}), f32[1,8,16]{2,0,1:T(1,128)S(1)}, u32[]{:S(2)}, u32[]{:S(2)}) async-start(f32[1,8,16]{2,0,1:T(1,128)} %bitcast.7), calls=%async_computation.1 | async-start | bytes 8192 | tf_op jit(solution)/shard_map/all_to_all | solution.py:91
  29.1 2.8 gather_fusion.17
  32.0 2.8 gather_fusion.23
  34.8 2.8 gather_fusion.11
  37.6 2.8 gather_fusion.5
  43.9 5.6 %all-to-all-start = ((f32[8,1,1024]{2,1,0:T(1,128)}), f32[8,1,1024]{2,1,0:T(1,128)S(1)}, u32[]{:S(2)}, u32[]{:S(2)}) async-start(f32[8,1,1024]{2,1,0:T(1,128)} %reshape.996), calls=%async_computation | async-start | bytes 65536 | tf_op jit(solution)/shard_map/all_to_all | solution.py:90
  51.6 3.4 all-to-all-done
  57.2 7.7 %psum.84 = f32[64]{0:T(128)S(1)} all-reduce(f32[64]{0:T(128)S(1)} %bitcast_reduce_fusion.3), channel_id=1, replica_groups=mesh['cells'=8,'ens'=4] {'ens'}, use_global_device_ids=true, to_apply=%region_4.7 | all-reduce | flops 64 | bytes 512 | tf_op jit(solution)/shard_map/psum | solution.py:98
  65.1 5.8 %psum.85 = f32[64]{0:T(128)S(1)} all-reduce(f32[64]{0:T(128)S(1)} %get-tuple-element.58), channel_id=1, replica_groups=mesh['cells'=8,'ens'=4] {'ens'}, use_global_device_ids=true, to_apply=%region_6.11 | all-reduce | flops 64 | bytes 512 | tf_op jit(solution)/shard_map/psum | solution.py:101
  71.3 24.7 %all_gather.12 = f32[67,512]{0,1:T(8,128)S(1)} all-gather(f32[67,64]{0,1:T(8,128)S(1)} %pad_maximum_fusion), channel_id=1, replica_groups=mesh['cells'=8,'ens'=4] {'cells'}, dimensions={1}, use_global_device_ids=true | all-gather | bytes 154368 | tf_op jit(solution)/shard_map/all_gather | solution.py:112
  99.8 36.4 %all-reduce.5.cloned.1.call-done = f32[4,96,512]{2,1,0:T(8,128)} async-done(((f32[4,96,512]{2,1,0:T(8,128)}), f32[4,96,512]{2,1,0:T(8,128)}) %all-reduce.5.cloned.1.call-update) | async-done | bytes 786448 | tf_op jit(solution)/shard_map/psum | solution.py:120
  139.9 5.6 %all-to-all-start.3 = ((f32[1,8,16]{2,0,1:T(1,128)}), f32[1,8,16]{2,0,1:T(1,128)S(1)}, u32[]{:S(2)}, u32[]{:S(2)}) async-start(f32[1,8,16]{2,0,1:T(1,128)} %bitcast.25), calls=%async_computation.3 | async-start | bytes 8192 | tf_op jit(solution)/shard_map/all_to_all | solution.py:91
  150.7 3.3 all-to-all-start.2
  155.6 3.9 all-to-all-done.2
  161.1 9.1 %psum.87 = f32[64]{0:T(128)S(1)} all-reduce(f32[64]{0:T(128)S(1)} %bitcast_reduce_fusion.2), channel_id=1, replica_groups=mesh['cells'=8,'ens'=4] {'ens'}, use_global_device_ids=true, to_apply=%region_13.20 | all-reduce | flops 64 | bytes 512 | tf_op jit(solution)/shard_map/psum | solution.py:98
  170.4 6.0 %psum.88 = f32[64]{0:T(128)S(1)} all-reduce(f32[64]{0:T(128)S(1)} %get-tuple-element.48), channel_id=1, replica_groups=mesh['cells'=8,'ens'=4] {'ens'}, use_global_device_ids=true, to_apply=%region_15.22 | all-reduce | flops 64 | bytes 512 | tf_op jit(solution)/shard_map/psum | solution.py:101
  176.8 24.9 %all_gather.13 = f32[67,512]{0,1:T(8,128)S(1)} all-gather(f32[67,64]{0,1:T(8,128)S(1)} %pad_maximum_fusion.1), channel_id=1, replica_groups=mesh['cells'=8,'ens'=4] {'cells'}, dimensions={1}, use_global_device_ids=true | all-gather | bytes 154368 | tf_op jit(solution)/shard_map/all_gather | solution.py:112
  205.6 35.6 %all-reduce.7.cloned.1.call-done = f32[4,96,512]{2,1,0:T(8,128)} async-done(((f32[4,96,512]{2,1,0:T(8,128)}), f32[4,96,512]{2,1,0:T(8,128)}) %all-reduce.7.cloned.1.call-update) | async-done | bytes 786448 | tf_op jit(solution)/shard_map/psum | solution.py:120
  244.9 5.6 %all-to-all-start.5 = ((f32[1,8,16]{2,0,1:T(1,128)}), f32[1,8,16]{2,0,1:T(1,128)S(1)}, u32[]{:S(2)}, u32[]{:S(2)}) async-start(f32[1,8,16]{2,0,1:T(1,128)} %bitcast.43), calls=%async_computation.5 | async-start | bytes 8192 | tf_op jit(solution)/shard_map/all_to_all | solution.py:91
  255.7 3.3 all-to-all-start.4
  260.6 3.9 all-to-all-done.4
  266.1 9.1 %psum.90 = f32[64]{0:T(128)S(1)} all-reduce(f32[64]{0:T(128)S(1)} %bitcast_reduce_fusion.1), channel_id=1, replica_groups=mesh['cells'=8,'ens'=4] {'ens'}, use_global_device_ids=true, to_apply=%region_22.29 | all-reduce | flops 64 | bytes 512 | tf_op jit(solution)/shard_map/psum | solution.py:98
  275.5 6.0 %psum.91 = f32[64]{0:T(128)S(1)} all-reduce(f32[64]{0:T(128)S(1)} %get-tuple-element.38), channel_id=1, replica_groups=mesh['cells'=8,'ens'=4] {'ens'}, use_global_device_ids=true, to_apply=%region_24.31 | all-reduce | flops 64 | bytes 512 | tf_op jit(solution)/shard_map/psum | solution.py:101
  281.8 24.7 %all_gather.14 = f32[67,512]{0,1:T(8,128)S(1)} all-gather(f32[67,64]{0,1:T(8,128)S(1)} %pad_maximum_fusion.2), channel_id=1, replica_groups=mesh['cells'=8,'ens'=4] {'cells'}, dimensions={1}, use_global_device_ids=true | all-gather | bytes 154368 | tf_op jit(solution)/shard_map/all_gather | solution.py:112
  310.5 35.6 %all-reduce.9.cloned.1.call-done = f32[4,96,512]{2,1,0:T(8,128)} async-done(((f32[4,96,512]{2,1,0:T(8,128)}), f32[4,96,512]{2,1,0:T(8,128)}) %all-reduce.9.cloned.1.call-update) | async-done | bytes 786448 | tf_op jit(solution)/shard_map/psum | solution.py:120
  349.7 5.6 %all-to-all-start.7 = ((f32[1,8,16]{2,0,1:T(1,128)}), f32[1,8,16]{2,0,1:T(1,128)S(1)}, u32[]{:S(2)}, u32[]{:S(2)}) async-start(f32[1,8,16]{2,0,1:T(1,128)} %bitcast.61), calls=%async_computation.7 | async-start | bytes 8192 | tf_op jit(solution)/shard_map/all_to_all | solution.py:91
  360.6 3.3 all-to-all-start.6
  365.5 3.9 all-to-all-done.6
  371.0 9.1 %psum.93 = f32[64]{0:T(128)S(1)} all-reduce(f32[64]{0:T(128)S(1)} %bitcast_reduce_fusion), channel_id=1, replica_groups=mesh['cells'=8,'ens'=4] {'ens'}, use_global_device_ids=true, to_apply=%region_31.38 | all-reduce | flops 64 | bytes 512 | tf_op jit(solution)/shard_map/psum | solution.py:98
  380.3 6.0 %psum.94 = f32[64]{0:T(128)S(1)} all-reduce(f32[64]{0:T(128)S(1)} %get-tuple-element.28), channel_id=1, replica_groups=mesh['cells'=8,'ens'=4] {'ens'}, use_global_device_ids=true, to_apply=%region_33.40 | all-reduce | flops 64 | bytes 512 | tf_op jit(solution)/shard_map/psum | solution.py:101
  386.7 24.9 %all_gather.15 = f32[67,512]{0,1:T(8,128)S(1)} all-gather(f32[67,64]{0,1:T(8,128)S(1)} %pad_maximum_fusion.3), channel_id=1, replica_groups=mesh['cells'=8,'ens'=4] {'cells'}, dimensions={1}, use_global_device_ids=true | all-gather | bytes 154368 | tf_op jit(solution)/shard_map/all_gather | solution.py:112
  415.4 35.7 %all-reduce.11.cloned.1.call-done = f32[4,96,512]{2,1,0:T(8,128)} async-done(((f32[4,96,512]{2,1,0:T(8,128)}), f32[4,96,512]{2,1,0:T(8,128)}) %all-reduce.11.cloned.1.call-update) | async-done | bytes 786448 | tf_op jit(solution)/shard_map/psum | solution.py:120
  (243 shorter events, 73.3 us)
Async XLA Ops:
  7.2 0.7 copy-start.8
  13.6 3.1 copy-start.6
  19.1 0.7 copy-start
  21.6 22.3 %all-to-all-start.1 = ((f32[1,8,16]{2,0,1:T(1,128)}), f32[1,8,16]{2,0,1:T(1,128)S(1)}, u32[]{:S(2)}, u32[]{:S(2)}) async-start(f32[1,8,16]{2,0,1:T(1,128)} %bitcast.7), calls=%async_computation.1 | async-start | bytes 8192 | tf_op jit(solution)/shard_map/all_to_all | solution.py:91
  28.0 0.7 copy-start.7
  37.6 4.5 copy-start.1
  43.9 5.6 %copy-start.9 = (s32[4,4]{1,0:T(4,128)S(1)}, s32[4,4]{1,0:T(4,128)}, u32[]{:S(2)}) copy-start(s32[4,4]{1,0:T(4,128)} %param.26) | copy-start | bytes 196
  43.9 11.1 %all-to-all-start = ((f32[8,1,1024]{2,1,0:T(1,128)}), f32[8,1,1024]{2,1,0:T(1,128)S(1)}, u32[]{:S(2)}, u32[]{:S(2)}) async-start(f32[8,1,1024]{2,1,0:T(1,128)} %reshape.996), calls=%async_computation | async-start | bytes 65536 | tf_op jit(solution)/shard_map/all_to_all | solution.py:90
  49.5 86.7 %all-reduce.5.cloned.1.call-start = ((), (), s32[]{:S(2)}) async-start(), calls=%async_computation.8 | async-start | bytes 1572864 | tf_op jit(solution)/shard_map/psum | solution.py:120
  56.4 8.5 %copy-start.10 = (f32[4,64]{1,0:T(4,128)S(1)}, f32[4,64]{1,0:T(4,128)}, u32[]{:S(2)}) copy-start(f32[4,64]{1,0:T(4,128)} %param.22) | copy-start | bytes 3076
  65.1 5.8 %copy-start.11 = (f32[4,64]{1,0:T(4,128)S(1)}, f32[4,64]{1,0:T(4,128)}, u32[]{:S(2)}) copy-start(f32[4,64]{1,0:T(4,128)} %param.23) | copy-start | bytes 3076
  136.2 9.3 %copy-start.4 = (f32[4,96,512]{2,1,0:T(8,128)S(1)}, f32[4,96,512]{2,1,0:T(8,128)}, u32[]{:S(2)}) copy-start(f32[4,96,512]{2,1,0:T(8,128)} %all-reduce.5.cloned.1.call-done) | copy-start | bytes 2359300
  139.9 10.8 %all-to-all-start.3 = ((f32[1,8,16]{2,0,1:T(1,128)}), f32[1,8,16]{2,0,1:T(1,128)S(1)}, u32[]{:S(2)}, u32[]{:S(2)}) async-start(f32[1,8,16]{2,0,1:T(1,128)} %bitcast.25), calls=%async_computation.3 | async-start | bytes 8192 | tf_op jit(solution)/shard_map/all_to_all | solution.py:91
  150.7 8.8 %all-to-all-start.2 = ((f32[8,1,1024]{2,1,0:T(1,128)}), f32[8,1,1024]{2,1,0:T(1,128)S(1)}, u32[]{:S(2)}, u32[]{:S(2)}) async-start(f32[8,1,1024]{2,1,0:T(1,128)} %reshape.998), calls=%async_computation.2 | async-start | bytes 65536 | tf_op jit(solution)/shard_map/all_to_all | solution.py:90
  154.1 87.2 %all-reduce.7.cloned.1.call-start = ((), (), s32[]{:S(2)}) async-start(), calls=%async_computation.9 | async-start | bytes 1572864 | tf_op jit(solution)/shard_map/psum | solution.py:120
  241.2 9.3 %copy-start.3 = (f32[4,96,512]{2,1,0:T(8,128)S(1)}, f32[4,96,512]{2,1,0:T(8,128)}, u32[]{:S(2)}) copy-start(f32[4,96,512]{2,1,0:T(8,128)} %all-reduce.7.cloned.1.call-done) | copy-start | bytes 2359300
  244.9 10.8 %all-to-all-start.5 = ((f32[1,8,16]{2,0,1:T(1,128)}), f32[1,8,16]{2,0,1:T(1,128)S(1)}, u32[]{:S(2)}, u32[]{:S(2)}) async-start(f32[1,8,16]{2,0,1:T(1,128)} %bitcast.43), calls=%async_computation.5 | async-start | bytes 8192 | tf_op jit(solution)/shard_map/all_to_all | solution.py:91
  255.7 8.8 %all-to-all-start.4 = ((f32[8,1,1024]{2,1,0:T(1,128)}), f32[8,1,1024]{2,1,0:T(1,128)S(1)}, u32[]{:S(2)}, u32[]{:S(2)}) async-start(f32[8,1,1024]{2,1,0:T(1,128)} %reshape.1000), calls=%async_computation.4 | async-start | bytes 65536 | tf_op jit(solution)/shard_map/all_to_all | solution.py:90
  259.1 87.0 %all-reduce.9.cloned.1.call-start = ((), (), s32[]{:S(2)}) async-start(), calls=%async_computation.10 | async-start | bytes 1572864 | tf_op jit(solution)/shard_map/psum | solution.py:120
  346.1 9.3 %copy-start.2 = (f32[4,96,512]{2,1,0:T(8,128)S(1)}, f32[4,96,512]{2,1,0:T(8,128)}, u32[]{:S(2)}) copy-start(f32[4,96,512]{2,1,0:T(8,128)} %all-reduce.9.cloned.1.call-done) | copy-start | bytes 2359300
  349.7 10.8 %all-to-all-start.7 = ((f32[1,8,16]{2,0,1:T(1,128)}), f32[1,8,16]{2,0,1:T(1,128)S(1)}, u32[]{:S(2)}, u32[]{:S(2)}) async-start(f32[1,8,16]{2,0,1:T(1,128)} %bitcast.61), calls=%async_computation.7 | async-start | bytes 8192 | tf_op jit(solution)/shard_map/all_to_all | solution.py:91
  360.6 8.8 %all-to-all-start.6 = ((f32[8,1,1024]{2,1,0:T(1,128)}), f32[8,1,1024]{2,1,0:T(1,128)S(1)}, u32[]{:S(2)}, u32[]{:S(2)}) async-start(f32[8,1,1024]{2,1,0:T(1,128)} %reshape.1002), calls=%async_computation.6 | async-start | bytes 65536 | tf_op jit(solution)/shard_map/all_to_all | solution.py:90
  363.9 87.2 %all-reduce.11.cloned.1.call-start = ((), (), s32[]{:S(2)}) async-start(), calls=%async_computation.11 | async-start | bytes 1572864 | tf_op jit(solution)/shard_map/psum | solution.py:120
  451.1 2.4 copy-start.5
Sparse Core Ops, SparseCore 0:
  99.0 37.1 all-reduce.4
  204.8 36.3 all-reduce.6
  309.6 36.3 all-reduce.8
  414.7 36.3 all-reduce.10
where the time goes:
time: 465 us; the launch traced here: 462 us
  waiting for transfers between devices  165 us (35%)
  blocking collectives  158 us (34%)
  local copies, waits for them, and re-layouts  47 us (10%)
  starting transfers between devices  38.9 us (8%)
  between operations  22.3 us (5%)
  other arithmetic  19.1 us (4%)
  matrix products  11.3 us (2%)
    psum x4, waiting for transfers between devices, shards(): cov_block = lax.psum(partial_cov, 'ens') / (MEMBERS - 1)  143 us
    all_gather x4, blocking collectives, shards(): gathered = lax.all_gather(panel, 'cells', axis=1, tiled=True)  99.3 us
    psum x4, blocking collectives, shards(): first_sum = lax.psum(jnp.sum(values, axis=0), 'ens')  35.1 us
    psum x4, blocking collectives, shards(): spread = lax.psum(jnp.sum(anomaly * anomaly, axis=0), 'ens') / (MEMBERS - 1)  23.7 us
    all_to_all x4, starting transfers between devices, shards(): lax.all_to_all(send_mean, 'cells', split_axis=1, concat_axis=1, tiled=True)  23.2 us
    all_to_all x4, starting transfers between devices, shards(): lax.all_to_all(send_pert, 'cells', split_axis=1, concat_axis=1, tiled=True)  15.6 us
    all_to_all x4, waiting for transfers between devices, shards(): lax.all_to_all(send_pert, 'cells', split_axis=1, concat_axis=1, tiled=True)  15.2 us
    gather x4, local copies, waits for them, and re-layouts, shards(): where_list = jnp.take(obs_where, flat_list).reshape(blk_per, list_len)  11.2 us
  transfers between devices with their start and end apart: 12, of which 11 were waited for; matrix products, arithmetic and copies ran while one was open for 7% of the time, Pallas kernels for 0%

commit v1 on v0

v1 whole, which is shorter than its diff:
```python
import functools

import jax
import jax.numpy as jnp
from jax import lax
from jax.experimental import pallas as pl
from jax.experimental.pallas import tpu as pltpu
from jax.sharding import PartitionSpec as P

MESH = pl.DeviceIdType.MESH
SLOTS = 32
LANES = 128


def split(x):
    hi = x.astype(jnp.bfloat16)
    return hi, (x - hi.astype(jnp.float32)).astype(jnp.bfloat16)


def dot(a, b, dims):
    return lax.dot_general(a, b, (dims, ((), ())), preferred_element_type=jnp.float32)


def dot3(a, b, dims):
    return dot(a[0], b[0], dims) + (dot(a[0], b[1], dims) + dot(a[1], b[0], dims))


def kernel(
    ncells,
    nens,
    order_ref,
    mean_ref,
    pert_ref,
    value_ref,
    error_ref,
    cell_ref,
    mean_out,
    pert_out,
    state,
    state_hi,
    state_lo,
    mean_own,
    obs_mine,
    obs_all,
    cell_own,
    rank_own,
    meta,
    panel,
    in_send,
    in_recv,
    obs_send,
    obs_recv,
    nb_send,
    nb_recv,
    out_send,
    out_recv,
    mout_send,
    mout_recv,
    local_sem,
):
    members, blk = state.shape
    mem_per = members // nens
    batches, obs_per = value_ref.shape
    ci = lax.axis_index("cells")
    ei = lax.axis_index("ens")
    odd = lax.rem(ci, 2)

    def place(e):
        return e + odd * (nens - 1 - 2 * e)

    k = place(ei)
    block = ci * nens + k
    last = ncells * nens - 1
    has_left = block > 0
    has_right = block < last

    barrier = pltpu.get_barrier_semaphore()
    for d in range(1, nens):
        pl.semaphore_signal(
            barrier, inc=1, device_id={"ens": lax.rem(ei + d, nens)}, device_id_type=MESH
        )

    def greet(d, carry):
        pl.semaphore_signal(
            barrier, inc=1, device_id={"cells": lax.rem(ci + d, ncells)}, device_id_type=MESH
        )
        return carry

    lax.fori_loop(1, ncells, greet, 0)

    obs_mine[0:batches, :] = value_ref[...]
    obs_mine[batches : 2 * batches, :] = error_ref[...]
    pl.semaphore_wait(barrier, nens - 1 + ncells - 1)

    def cols(block_k):
        return pl.ds(pl.multiple_of(block_k * blk, blk), blk)

    def rows(e):
        return pl.ds(pl.multiple_of(e * mem_per, mem_per), mem_per)

    in_copies = []
    for d in range(1, nens):
        to = lax.rem(ei + d, nens)
        in_copies.append(
            pltpu.make_async_remote_copy(
                src_ref=pert_ref.at[:, cols(place(to))],
                dst_ref=state.at[rows(ei), :],
                send_sem=in_send.at[d],
                recv_sem=in_recv.at[d],
                device_id={"ens": to},
                device_id_type=MESH,
            )
        )
    for c in in_copies:
        c.start()
    own_in = pltpu.make_async_copy(
        pert_ref.at[:, cols(k)], state.at[rows(ei), :], local_sem.at[0]
    )
    own_in.start()

    def obs_copy(d):
        return pltpu.make_async_remote_copy(
            src_ref=obs_mine,
            dst_ref=obs_all.at[ci],
            send_sem=obs_send.at[d],
            recv_sem=obs_recv.at[d],
            device_id={"cells": lax.rem(ci + d, ncells)},
            device_id_type=MESH,
        )

    def obs_start(d, carry):
        obs_copy(d).start()
        return carry

    lax.fori_loop(1, ncells, obs_start, 0)
    own_obs = pltpu.make_async_copy(obs_mine, obs_all.at[ci], local_sem.at[1])
    own_obs.start()

    lane_a = lax.broadcasted_iota(jnp.int32, (obs_per, obs_per), 0)
    lane_b = lax.broadcasted_iota(jnp.int32, (obs_per, obs_per), 1)
    earlier = (lane_a < lane_b).astype(jnp.bfloat16)
    run = jnp.zeros((batches, 1), jnp.float32)
    for o in range(ncells):
        cells = cell_ref[:, o * obs_per : (o + 1) * obs_per]
        inside = (cells >= block * blk) & (cells < (block + 1) * blk)
        ones = jnp.where(inside, 1.0, 0.0)
        before = dot(ones.astype(jnp.bfloat16), earlier, ((1,), (0,)))
        cell_own[o] = cells
        rank_own[o] = jnp.where(inside, (before + run).astype(jnp.int32), -1)
        run = run + jnp.sum(ones, axis=1, keepdims=True)

    mean_own[...] = mean_ref[:, cols(k)]

    @pl.when(jnp.logical_not(has_left))
    def _():
        for t in range(batches):
            panel[t, 0] = jnp.zeros(panel.shape[2:], jnp.float32)

    @pl.when(jnp.logical_not(has_right))
    def _():
        for t in range(batches):
            panel[t, 2] = jnp.zeros(panel.shape[2:], jnp.float32)

    def obs_wait(d, carry):
        obs_copy(d).wait()
        return carry

    own_obs.wait()
    lax.fori_loop(1, ncells, obs_wait, 0)

    slot_ids = lax.broadcasted_iota(jnp.int32, (SLOTS, obs_per), 0)
    lane_ids = lax.broadcasted_iota(jnp.int32, (SLOTS, LANES), 1)
    for b in range(batches):

        def pick(o, acc):
            hit = rank_own[o, b : b + 1, :] == slot_ids
            cell = cell_own[o, b : b + 1, :]
            value = obs_all[o, b : b + 1, :]
            error = obs_all[o, batches + b : batches + b + 1, :]
            return (
                acc[0] + jnp.where(hit, cell + 1, 0),
                acc[1] + jnp.where(hit, value, 0.0),
                acc[2] + jnp.where(hit, error, 0.0),
            )

        zero = jnp.zeros((SLOTS, obs_per), jnp.float32)
        acc = lax.fori_loop(0, ncells, pick, (zero.astype(jnp.int32), zero, zero), unroll=min(ncells, 8))
        cell = jnp.sum(acc[0].astype(jnp.float32), axis=1, keepdims=True) - 1.0
        value = jnp.sum(acc[1], axis=1, keepdims=True)
        error = jnp.sum(acc[2], axis=1, keepdims=True)
        meta[b] = jnp.where(lane_ids == 0, cell, jnp.where(lane_ids == 1, value, error))

    for c in in_copies:
        c.wait()
    own_in.wait()
    for h in range(0, blk, 256):
        hi, lo = split(state[:, h : h + 256])
        state_hi[:, h : h + 256] = hi
        state_lo[:, h : h + 256] = lo

    left_c = jnp.where(k > 0, ci, ci - 1)
    left_e = jnp.where(k > 0, place(k - 1), ei)
    right_c = jnp.where(k < nens - 1, ci, ci + 1)
    right_e = jnp.where(k < nens - 1, place(k + 1), ei)

    width = 256
    for t in range(batches):
        b = order_ref[t]
        info = meta[b]
        cell = info[:, 0:1]
        value = info[:, 1:2]
        live = cell >= 0.0
        error = jnp.where(live, info[:, 2:3], 1.0)
        ids = lax.broadcasted_iota(jnp.int32, (SLOTS, blk), 1) + block * blk
        here = ids == cell.astype(jnp.int32)
        onehot = jnp.where(here, 1.0, 0.0).astype(jnp.bfloat16)
        values = dot(onehot, state_hi[...], ((1,), (1,))) + dot(
            onehot, state_lo[...], ((1,), (1,))
        )
        base = jnp.sum(jnp.where(here, mean_own[...], 0.0), axis=1, keepdims=True)
        shift = jnp.sum(values, axis=1, keepdims=True) / members
        anomaly = values - shift
        spread = jnp.sum(anomaly * anomaly, axis=1, keepdims=True) / (members - 1)
        innovation = value - (base + shift)
        total = spread + error
        gain = jnp.where(live, 1.0 / total, 0.0)
        alpha = 1.0 / (1.0 + jnp.sqrt(error / total))
        panel[t, 1, :, 0:members] = anomaly
        panel[t, 1, :, members : members + LANES] = jnp.where(
            lane_ids == 0,
            innovation,
            jnp.where(lane_ids == 1, gain, jnp.where(lane_ids == 2, alpha, cell)),
        )
        to_left = pltpu.make_async_remote_copy(
            src_ref=panel.at[t, 1],
            dst_ref=panel.at[t, 2],
            send_sem=nb_send.at[t, 0],
            recv_sem=nb_recv.at[t, 2],
            device_id={"cells": left_c, "ens": left_e},
            device_id_type=MESH,
        )
        to_right = pltpu.make_async_remote_copy(
            src_ref=panel.at[t, 1],
            dst_ref=panel.at[t, 0],
            send_sem=nb_send.at[t, 1],
            recv_sem=nb_recv.at[t, 0],
            device_id={"cells": right_c, "ens": right_e},
            device_id_type=MESH,
        )

        @pl.when(has_left)
        def _():
            to_left.start()

        @pl.when(has_right)
        def _():
            to_right.start()

        @pl.when(has_left)
        def _():
            to_left.wait_send()
            to_right.wait_recv()

        @pl.when(has_right)
        def _():
            to_right.wait_send()
            to_left.wait_recv()

        sel = jnp.concatenate([panel[t, s, :, 0:members] for s in range(3)], axis=0)
        facts = jnp.concatenate(
            [panel[t, s, :, members : members + LANES] for s in range(3)], axis=0
        )
        sel_parts = split(sel)
        sel_t = split(sel.T)
        innov_l = facts[:, 0:1]
        gain_l = facts[:, 1:2] / (members - 1)
        alpha_l = facts[:, 2:3]
        cell_l = facts[:, 3:4]
        for h in range(0, blk, width):
            at = slice(h, h + width)
            cov = dot3(sel_parts, (state_hi[:, at], state_lo[:, at]), ((1,), (0,)))
            ids = lax.broadcasted_iota(jnp.int32, (3 * SLOTS, width), 1) + (block * blk + h)
            f = jnp.abs(ids.astype(jnp.float32) - cell_l) * (1.0 / (2 * blk))
            taper = jnp.where(f < 1.0, (1.0 - f) * (1.0 - f) * (1.0 + 2.0 * f), 0.0)
            weight = cov * taper * gain_l
            mean_own[:, at] = mean_own[:, at] + jnp.sum(weight * innov_l, axis=0, keepdims=True)
            update = dot3(sel_t, split(weight * alpha_l), ((1,), (0,)))
            new = state[:, at] - update
            state[:, at] = new
            if t < batches - 1:
                hi, lo = split(new)
                state_hi[:, at] = hi
                state_lo[:, at] = lo

    out_copies = []
    for d in range(1, nens):
        to = lax.rem(ei + d, nens)
        out_copies.append(
            pltpu.make_async_remote_copy(
                src_ref=state.at[rows(to), :],
                dst_ref=pert_out.at[:, cols(k)],
                send_sem=out_send.at[d],
                recv_sem=out_recv.at[d],
                device_id={"ens": to},
                device_id_type=MESH,
            )
        )
        out_copies.append(
            pltpu.make_async_remote_copy(
                src_ref=mean_own,
                dst_ref=mean_out.at[:, cols(k)],
                send_sem=mout_send.at[d],
                recv_sem=mout_recv.at[d],
                device_id={"ens": to},
                device_id_type=MESH,
            )
        )
    for c in out_copies:
        c.start()
    own_out = [
        pltpu.make_async_copy(state.at[rows(ei), :], pert_out.at[:, cols(k)], local_sem.at[2]),
        pltpu.make_async_copy(mean_own, mean_out.at[:, cols(k)], local_sem.at[3]),
    ]
    for c in own_out:
        c.start()
    for c in own_out + out_copies:
        c.wait()


def shards(ncells, nens, mean, pert, value, error, cell, block_obs, block_count, order):
    mem_per, cell_per = pert.shape
    members = mem_per * nens
    batches, obs_per = value.shape
    blk = cell_per // block_obs.shape[1]
    vmem = pl.BlockSpec(memory_space=pltpu.VMEM)
    smem = pl.BlockSpec(memory_space=pltpu.SMEM)
    anywhere = pl.BlockSpec(memory_space=pl.ANY)
    mean_new, pert_new = pl.pallas_call(
        functools.partial(kernel, ncells, nens),
        out_shape=(
            jax.ShapeDtypeStruct((1, cell_per), jnp.float32),
            jax.ShapeDtypeStruct((mem_per, cell_per), jnp.float32),
        ),
        in_specs=[smem, vmem, anywhere, vmem, vmem, vmem],
        out_specs=(vmem, anywhere),
        scratch_shapes=[
            pltpu.VMEM((members, blk), jnp.float32),
            pltpu.VMEM((members, blk), jnp.bfloat16),
            pltpu.VMEM((members, blk), jnp.bfloat16),
            pltpu.VMEM((1, blk), jnp.float32),
            pltpu.VMEM((2 * batches, obs_per), jnp.float32),
            pltpu.VMEM((ncells, 2 * batches, obs_per), jnp.float32),
            pltpu.VMEM((ncells, batches, obs_per), jnp.int32),
            pltpu.VMEM((ncells, batches, obs_per), jnp.int32),
            pltpu.VMEM((batches, SLOTS, LANES), jnp.float32),
            pltpu.VMEM((batches, 3, SLOTS, members + LANES), jnp.float32),
            pltpu.SemaphoreType.DMA((nens,)),
            pltpu.SemaphoreType.DMA((nens,)),
            pltpu.SemaphoreType.DMA((ncells,)),
            pltpu.SemaphoreType.DMA((ncells,)),
            pltpu.SemaphoreType.DMA((batches, 2)),
            pltpu.SemaphoreType.DMA((batches, 3)),
            pltpu.SemaphoreType.DMA((nens,)),
            pltpu.SemaphoreType.DMA((nens,)),
            pltpu.SemaphoreType.DMA((nens,)),
            pltpu.SemaphoreType.DMA((nens,)),
            pltpu.SemaphoreType.DMA((4,)),
        ],
        compiler_params=pltpu.CompilerParams(
            collective_id=0, has_side_effects=True, vmem_limit_bytes=32 * 1024 * 1024
        ),
    )(order, mean.reshape(1, cell_per), pert, value, error, cell)
    return mean_new.reshape(cell_per), pert_new


def solution(mesh):
    placed = (
        P("cells"),
        P("ens", "cells"),
        P(None, "cells"),
        P(None, "cells"),
        P(),
        P(None, "cells", None),
        P(None, "cells"),
        P(),
    )
    return jax.shard_map(
        functools.partial(shards, mesh.shape["cells"], mesh.shape["ens"]),
        mesh=mesh,
        in_specs=placed,
        out_specs=(P("cells"), P("ens", "cells")),
        check_vma=False,
    )
```

time: 465 us -> 42.5 us (0.09)
  waiting for transfers between devices: 165 us -> 0 us
  blocking collectives: 158 us -> 0 us
  local copies, waits for them, and re-layouts: 47 us -> 5.84 us
  starting transfers between devices: 38.9 us -> 0 us
  Pallas kernels: 0 us -> 35.6 us
  between operations: 22.3 us -> 0.65 us
  other arithmetic: 19.1 us -> 0 us
  matrix products: 11.3 us -> 0 us
    psum x4 -> x0, waiting for transfers between devices: 143 us -> none  [shards(): cov_block = lax.psum(partial_cov, 'ens') / (MEMBERS - 1)]
    all_gather x4 -> x0, blocking collectives: 99.3 us -> none  [shards(): gathered = lax.all_gather(panel, 'cells', axis=1, tiled=True)]
    psum x8 -> x0, blocking collectives: 58.8 us -> none  [the longest x4 35.1 us: shards(): first_sum = lax.psum(jnp.sum(values, axis=0), 'ens')]
    all_to_all x8 -> x0, starting transfers between devices: 38.8 us -> none  [the longest x4 23.2 us: shards(): lax.all_to_all(send_mean, 'cells', split_axis=1, concat_axis=1, tiled=True)]
    pallas_call x0 -> x1, Pallas kernels: none -> 35.6 us  [shards(): pl.pallas_call(functools.partial(kernel, ncells, nens), out_shape=(jax.Sh...]
    gather x24 -> x0, local copies, waits for them, and re-layouts: 28.3 us -> none  [the longest x4 11.2 us: shards(): where_list = jnp.take(obs_where, flat_list).reshape(blk_per, list_len)]
    all_to_all x8 -> x0, waiting for transfers between devices: 22 us -> none  [the longest x4 15.2 us: shards(): lax.all_to_all(send_pert, 'cells', split_axis=1, concat_axis=1, tiled=True)]
    dot_general x8 -> x0, matrix products: 11.3 us -> none  [the longest x4 6.7 us: shards(): jnp.einsum('mbl,mbc->blc', sel_anoms, blocks, precision=lax.Precision.HIG...]
  transfers between devices with their start and end apart: 12 -> 0, of which waited for: 11 -> 0; matrix products, arithmetic and copies ran while one was open for 7% -> 0% of each run, Pallas kernels for 0% -> 0%
where the time goes in v1:
time: 42.5 us; the launch traced here: 42.1 us
  Pallas kernels  35.6 us (84%)
  local copies, waits for them, and re-layouts  5.84 us (14%)
  between operations  0.65 us (2%)
    pallas_call x1, Pallas kernels, shards(): pl.pallas_call(functools.partial(kernel, ncells, nens), out_shape=(jax.Sh...  35.6 us
    unnamed x14, local copies, waits for them, and re-layouts  5.84 us

profile of v1, /device:TPU:1, one launch (start us, length us, event | category | flops | bytes accessed | tf_op | source)
XLA Modules:
  0.0 42.1 jit_solution(18213719106303904170)
XLA Ops:
  0.6 0.0 copy-start.5
  0.6 0.6 %copy-done.5 = s32[4]{0:T(128)S(1)} copy-done((s32[4]{0:T(128)S(1)}, s32[4]{0:T(128)}, u32[]{:S(2)}) %copy-start.5) | copy-done | bytes 40
  1.3 0.0 copy-start
  1.3 1.0 %copy-done = f32[64,2048]{1,0:T(8,128)S(1)} copy-done((f32[64,2048]{1,0:T(8,128)S(1)}, f32[64,2048]{1,0:T(8,128)}, u32[]{:S(2)}) %copy-start) | copy-done | bytes 524312
  2.3 0.0 copy-start.1
  2.3 0.7 %copy-done.1 = f32[2048]{0:T(1024)S(1)} copy-done((f32[2048]{0:T(1024)S(1)}, f32[2048]{0:T(1024)}, u32[]{:S(2)}) %copy-start.1) | copy-done | bytes 8216
  3.0 0.0 copy-start.2
  3.0 0.7 %copy-done.2 = s32[4,512]{1,0:T(4,128)S(1)} copy-done((s32[4,512]{1,0:T(4,128)S(1)}, s32[4,512]{1,0:T(4,128)}, u32[]{:S(2)}) %copy-start.2) | copy-done | bytes 8216
  3.7 0.0 copy-start.3
  3.7 0.7 %copy-done.3 = f32[4,64]{1,0:T(4,128)S(1)} copy-done((f32[4,64]{1,0:T(4,128)S(1)}, f32[4,64]{1,0:T(4,128)}, u32[]{:S(2)}) %copy-start.3) | copy-done | bytes 1048
  4.4 0.0 copy-start.4
  4.4 0.7 %copy-done.4 = f32[4,64]{1,0:T(4,128)S(1)} copy-done((f32[4,64]{1,0:T(4,128)S(1)}, f32[4,64]{1,0:T(4,128)}, u32[]{:S(2)}) %copy-start.4) | copy-done | bytes 1048
  5.1 35.6 %shard_map.77 = (f32[1,2048]{1,0:T(1,128)S(1)}, f32[64,2048]{1,0:T(8,128)S(1)}) custom-call(s32[4]{0:T(128)S(1)} %copy-done.5, f32[1,2048]{1,0:T(1,128)S(1)} %bitcast.2, f32[64,2048]{1,0:T(8,128)S(1)} %copy-done, f32[4,64]{1,0:T(4,128)S(1)} %copy-done.3, f32[4,64]{1,0:T(4,128)S(1)} %copy-done.4, s32[4,512]{1,0:T(4,128)S(1)} %copy-done.2), custom_call_target="tpu_custom_call" | custom-call | tf_op jit(solution)/shard_map/pallas_call | solution.py:338
  40.7 0.6 %copy.10 = f32[2048]{0:T(1024)} copy(f32[2048]{0:T(1024)S(1)} %bitcast.3) | data formatting | bytes 16384
  41.3 0.8 %copy.11 = f32[64,2048]{1,0:T(8,128)} copy(f32[64,2048]{1,0:T(8,128)S(1)} %get-tuple-element.9) | data formatting | bytes 1048576
Async XLA Ops:
  0.6 0.7 %copy-start.5 = (s32[4]{0:T(128)S(1)}, s32[4]{0:T(128)}, u32[]{:S(2)}) copy-start(s32[4]{0:T(128)} %order_ref.1) | copy-start | bytes 52
  1.3 1.0 %copy-start = (f32[64,2048]{1,0:T(8,128)S(1)}, f32[64,2048]{1,0:T(8,128)}, u32[]{:S(2)}) copy-start(f32[64,2048]{1,0:T(8,128)} %pert_ref.1) | copy-start | bytes 1572868
  2.3 0.7 %copy-start.1 = (f32[2048]{0:T(1024)S(1)}, f32[2048]{0:T(1024)}, u32[]{:S(2)}) copy-start(f32[2048]{0:T(1024)} %param.8) | copy-start | bytes 24580
  3.0 0.7 %copy-start.2 = (s32[4,512]{1,0:T(4,128)S(1)}, s32[4,512]{1,0:T(4,128)}, u32[]{:S(2)}) copy-start(s32[4,512]{1,0:T(4,128)} %cell_ref.1) | copy-start | bytes 24580
  3.7 0.7 %copy-start.3 = (f32[4,64]{1,0:T(4,128)S(1)}, f32[4,64]{1,0:T(4,128)}, u32[]{:S(2)}) copy-start(f32[4,64]{1,0:T(4,128)} %value_ref.1) | copy-start | bytes 3076
  4.4 0.7 %copy-start.4 = (f32[4,64]{1,0:T(4,128)S(1)}, f32[4,64]{1,0:T(4,128)}, u32[]{:S(2)}) copy-start(f32[4,64]{1,0:T(4,128)} %error_ref.1) | copy-start | bytes 3076

commit v2 on v1

--- a/solution.py
+++ b/solution.py
@@ -33,13 +33,14 @@
     pert_ref,
     value_ref,
     error_ref,
-    cell_ref,
+    cell_hbm,
     mean_out,
     pert_out,
     state,
     state_hi,
     state_lo,
     mean_own,
+    cell_ref,
     obs_mine,
     obs_all,
     cell_own,
@@ -74,6 +75,17 @@
     has_left = block > 0
     has_right = block < last
 
+    def cols(block_k):
+        return pl.ds(pl.multiple_of(block_k * blk, blk), blk)
+
+    loads = [
+        pltpu.make_async_copy(value_ref, obs_mine.at[0:batches, :], local_sem.at[4]),
+        pltpu.make_async_copy(error_ref, obs_mine.at[batches : 2 * batches, :], local_sem.at[5]),
+        pltpu.make_async_copy(cell_hbm, cell_ref, local_sem.at[6]),
+        pltpu.make_async_copy(mean_ref.at[:, cols(k)], mean_own, local_sem.at[7]),
+    ]
+    for c in loads:
+        c.start()
     barrier = pltpu.get_barrier_semaphore()
     for d in range(1, nens):
         pl.semaphore_signal(
@@ -88,12 +100,7 @@
 
     lax.fori_loop(1, ncells, greet, 0)
 
-    obs_mine[0:batches, :] = value_ref[...]
-    obs_mine[batches : 2 * batches, :] = error_ref[...]
     pl.semaphore_wait(barrier, nens - 1 + ncells - 1)
-
-    def cols(block_k):
-        return pl.ds(pl.multiple_of(block_k * blk, blk), blk)
 
     def rows(e):
         return pl.ds(pl.multiple_of(e * mem_per, mem_per), mem_per)
@@ -117,6 +124,8 @@
         pert_ref.at[:, cols(k)], state.at[rows(ei), :], local_sem.at[0]
     )
     own_in.start()
+    for c in loads:
+        c.wait()
 
     def obs_copy(d):
         return pltpu.make_async_remote_copy(
@@ -149,8 +158,6 @@
         rank_own[o] = jnp.where(inside, (before + run).astype(jnp.int32), -1)
         run = run + jnp.sum(ones, axis=1, keepdims=True)
 
-    mean_own[...] = mean_ref[:, cols(k)]
-
     @pl.when(jnp.logical_not(has_left))
     def _():
         for t in range(batches):
@@ -204,6 +211,7 @@
     right_e = jnp.where(k < nens - 1, place(k + 1), ei)
 
     width = 256
+    out_copies, own_out = [], []
     for t in range(batches):
         b = order_ref[t]
         info = meta[b]
@@ -291,38 +299,43 @@
                 hi, lo = split(new)
                 state_hi[:, at] = hi
                 state_lo[:, at] = lo
-
-    out_copies = []
+                continue
+            part = h // width
+            there = pl.ds(pl.multiple_of(k * blk + h, width), width)
+            for d in range(1, nens):
+                to = lax.rem(ei + d, nens)
+                out_copies.append(
+                    pltpu.make_async_remote_copy(
+                        src_ref=state.at[rows(to), pl.ds(h, width)],
+                        dst_ref=pert_out.at[:, there],
+                        send_sem=out_send.at[part, d],
+                        recv_sem=out_recv.at[part, d],
+                        device_id={"ens": to},
+                        device_id_type=MESH,
+                    )
+                )
+                out_copies[-1].start()
+            own_out.append(
+                pltpu.make_async_copy(
+                    state.at[rows(ei), pl.ds(h, width)], pert_out.at[:, there], local_sem.at[8 + part]
+                )
+            )
+            own_out[-1].start()
+
     for d in range(1, nens):
-        to = lax.rem(ei + d, nens)
-        out_copies.append(
-            pltpu.make_async_remote_copy(
-                src_ref=state.at[rows(to), :],
-                dst_ref=pert_out.at[:, cols(k)],
-                send_sem=out_send.at[d],
-                recv_sem=out_recv.at[d],
-                device_id={"ens": to},
-                device_id_type=MESH,
-            )
-        )
         out_copies.append(
             pltpu.make_async_remote_copy(
                 src_ref=mean_own,
                 dst_ref=mean_out.at[:, cols(k)],
                 send_sem=mout_send.at[d],
                 recv_sem=mout_recv.at[d],
-                device_id={"ens": to},
+                device_id={"ens": lax.rem(ei + d, nens)},
                 device_id_type=MESH,
             )
         )
-    for c in out_copies:
-        c.start()
-    own_out = [
-        pltpu.make_async_copy(state.at[rows(ei), :], pert_out.at[:, cols(k)], local_sem.at[2]),
-        pltpu.make_async_copy(mean_own, mean_out.at[:, cols(k)], local_sem.at[3]),
-    ]
-    for c in own_out:
-        c.start()
+        out_copies[-1].start()
+    own_out.append(pltpu.make_async_copy(mean_own, mean_out.at[:, cols(k)], local_sem.at[3]))
+    own_out[-1].start()
     for c in own_out + out_copies:
         c.wait()
 
@@ -334,6 +347,7 @@
     blk = cell_per // block_obs.shape[1]
     vmem = pl.BlockSpec(memory_space=pltpu.VMEM)
     smem = pl.BlockSpec(memory_space=pltpu.SMEM)
+    hbm = pl.BlockSpec(memory_space=pltpu.HBM)
     anywhere = pl.BlockSpec(memory_space=pl.ANY)
     mean_new, pert_new = pl.pallas_call(
         functools.partial(kernel, ncells, nens),
@@ -341,13 +355,14 @@
             jax.ShapeDtypeStruct((1, cell_per), jnp.float32),
             jax.ShapeDtypeStruct((mem_per, cell_per), jnp.float32),
         ),
-        in_specs=[smem, vmem, anywhere, vmem, vmem, vmem],
+        in_specs=[smem] + [hbm] * 5,
         out_specs=(vmem, anywhere),
         scratch_shapes=[
             pltpu.VMEM((members, blk), jnp.float32),
             pltpu.VMEM((members, blk), jnp.bfloat16),
             pltpu.VMEM((members, blk), jnp.bfloat16),
             pltpu.VMEM((1, blk), jnp.float32),
+            pltpu.VMEM(cell.shape, jnp.int32),
             pltpu.VMEM((2 * batches, obs_per), jnp.float32),
             pltpu.VMEM((ncells, 2 * batches, obs_per), jnp.float32),
             pltpu.VMEM((ncells, batches, obs_per), jnp.int32),
@@ -360,11 +375,11 @@
             pltpu.SemaphoreType.DMA((ncells,)),
             pltpu.SemaphoreType.DMA((batches, 2)),
             pltpu.SemaphoreType.DMA((batches, 3)),
+            pltpu.SemaphoreType.DMA((blk // 256, nens)),
+            pltpu.SemaphoreType.DMA((blk // 256, nens)),
             pltpu.SemaphoreType.DMA((nens,)),
             pltpu.SemaphoreType.DMA((nens,)),
-            pltpu.SemaphoreType.DMA((nens,)),
-            pltpu.SemaphoreType.DMA((nens,)),
-            pltpu.SemaphoreType.DMA((4,)),
+            pltpu.SemaphoreType.DMA((8 + blk // 256,)),
         ],
         compiler_params=pltpu.CompilerParams(
             collective_id=0, has_side_effects=True, vmem_limit_bytes=32 * 1024 * 1024

time: 42.5 us -> 43.1 us (1.014)
  no operation moved by 1% of the time
where the time goes in v2:
time: 43.1 us; the launch traced here: 42.5 us
  Pallas kernels  36 us (84%)
  local copies, waits for them, and re-layouts  5.84 us (14%)
  between operations  0.65 us (2%)
    pallas_call x1, Pallas kernels, shards(): pl.pallas_call(functools.partial(kernel, ncells, nens), out_shape=(jax.Sh...  36 us
    unnamed x14, local copies, waits for them, and re-layouts  5.84 us

profile of v2, /device:TPU:1, one launch (start us, length us, event | category | flops | bytes accessed | tf_op | source)
XLA Modules:
  0.0 42.5 jit_solution(16515366463331646309)
XLA Ops:
  0.6 0.0 copy-start.5
  0.6 0.6 %copy-done.5 = s32[4]{0:T(128)S(1)} copy-done((s32[4]{0:T(128)S(1)}, s32[4]{0:T(128)}, u32[]{:S(2)}) %copy-start.5) | copy-done | bytes 40
  1.3 0.0 copy-start
  1.3 1.0 %copy-done = f32[64,2048]{1,0:T(8,128)S(1)} copy-done((f32[64,2048]{1,0:T(8,128)S(1)}, f32[64,2048]{1,0:T(8,128)}, u32[]{:S(2)}) %copy-start) | copy-done | bytes 524312
  2.3 0.0 copy-start.1
  2.3 0.7 %copy-done.1 = f32[2048]{0:T(1024)S(1)} copy-done((f32[2048]{0:T(1024)S(1)}, f32[2048]{0:T(1024)}, u32[]{:S(2)}) %copy-start.1) | copy-done | bytes 8216
  3.0 0.0 copy-start.2
  3.0 0.7 %copy-done.2 = s32[4,512]{1,0:T(4,128)S(1)} copy-done((s32[4,512]{1,0:T(4,128)S(1)}, s32[4,512]{1,0:T(4,128)}, u32[]{:S(2)}) %copy-start.2) | copy-done | bytes 8216
  3.7 0.0 copy-start.3
  3.7 0.7 %copy-done.3 = f32[4,64]{1,0:T(4,128)S(1)} copy-done((f32[4,64]{1,0:T(4,128)S(1)}, f32[4,64]{1,0:T(4,128)}, u32[]{:S(2)}) %copy-start.3) | copy-done | bytes 1048
  4.4 0.0 copy-start.4
  4.4 0.7 %copy-done.4 = f32[4,64]{1,0:T(4,128)S(1)} copy-done((f32[4,64]{1,0:T(4,128)S(1)}, f32[4,64]{1,0:T(4,128)}, u32[]{:S(2)}) %copy-start.4) | copy-done | bytes 1048
  5.1 36.0 %shard_map.77 = (f32[1,2048]{1,0:T(1,128)S(1)}, f32[64,2048]{1,0:T(8,128)S(1)}) custom-call(s32[4]{0:T(128)S(1)} %copy-done.5, f32[1,2048]{1,0:T(1,128)S(1)} %bitcast.2, f32[64,2048]{1,0:T(8,128)S(1)} %copy-done, f32[4,64]{1,0:T(4,128)S(1)} %copy-done.3, f32[4,64]{1,0:T(4,128)S(1)} %copy-done.4, s32[4,512]{1,0:T(4,128)S(1)} %copy-done.2), custom_call_target="tpu_custom_call" | custom-call | tf_op jit(solution)/shard_map/pallas_call | solution.py:352
  41.1 0.6 %copy.10 = f32[2048]{0:T(1024)} copy(f32[2048]{0:T(1024)S(1)} %bitcast.3) | data formatting | bytes 16384
  41.7 0.8 %copy.11 = f32[64,2048]{1,0:T(8,128)} copy(f32[64,2048]{1,0:T(8,128)S(1)} %get-tuple-element.9) | data formatting | bytes 1048576
Async XLA Ops:
  0.6 0.7 %copy-start.5 = (s32[4]{0:T(128)S(1)}, s32[4]{0:T(128)}, u32[]{:S(2)}) copy-start(s32[4]{0:T(128)} %order_ref.1) | copy-start | bytes 52
  1.3 1.0 %copy-start = (f32[64,2048]{1,0:T(8,128)S(1)}, f32[64,2048]{1,0:T(8,128)}, u32[]{:S(2)}) copy-start(f32[64,2048]{1,0:T(8,128)} %pert_ref.1) | copy-start | bytes 1572868
  2.3 0.7 %copy-start.1 = (f32[2048]{0:T(1024)S(1)}, f32[2048]{0:T(1024)}, u32[]{:S(2)}) copy-start(f32[2048]{0:T(1024)} %param.8) | copy-start | bytes 24580
  3.0 0.7 %copy-start.2 = (s32[4,512]{1,0:T(4,128)S(1)}, s32[4,512]{1,0:T(4,128)}, u32[]{:S(2)}) copy-start(s32[4,512]{1,0:T(4,128)} %cell_hbm.1) | copy-start | bytes 24580
  3.7 0.7 %copy-start.3 = (f32[4,64]{1,0:T(4,128)S(1)}, f32[4,64]{1,0:T(4,128)}, u32[]{:S(2)}) copy-start(f32[4,64]{1,0:T(4,128)} %value_ref.1) | copy-start | bytes 3076
  4.4 0.7 %copy-start.4 = (f32[4,64]{1,0:T(4,128)S(1)}, f32[4,64]{1,0:T(4,128)}, u32[]{:S(2)}) copy-start(f32[4,64]{1,0:T(4,128)} %error_ref.1) | copy-start | bytes 3076
